TPU v7x, 128 devices: a whole 4x4x4 slice. The times are simulated.
128 devices in a mesh: row: 16 (over x_lo, y, core), col: 8 (over x_hi, z).
Axes of the slice: x: 4 (x_hi: 2, x_lo: 2; x = x_hi * 2 + x_lo), y: 4, z: 4, core: 2. Of those that a mesh axis runs over, the one named last changes fastest.
Arguments:
- item_embed: float32 [131072, 128], P(('col', 'row')), may hold values from -6 to 6
- item_degree: int32 [131072], P(('col', 'row')), may hold values from 1 to 64
- cotangent: float32 [131072, 128], P(('row', 'col')), may hold values from -6 to 6
- user_degree: int32 [131072], P(('row', 'col')), may hold values from 1 to 64
- tile_values: bfloat16 [128, 384, 128, 128], P(('row', 'col')), may hold values from 0.049804688 to 1
- tile_slots: int32 [128, 384], P(('row', 'col')), may hold values from 0 to 8191, as said below
- tile_count: int32 [128], P(('row', 'col')), may hold values from 48 to 384, as said below
Outputs:
- user_out: float32 [131072, 128], P(('row', 'col'))
- item_grad: float32 [131072, 128], P(('col', 'row'))
Inputs may be any that keep to these rules, and one draw needn't show every extreme that they name: `tile_slots`: the 384 slots of one device are distinct. `tile_count`: one device has exactly 384 live slots.
All inputs are finite; a program needn't handle non-finite values.
Results may differ from a plain program's by a relative error of at most 0.0029.
Values may be sent and summed in bfloat16 or wider, within the bound.
No kernel may reach another device: no remote copies, remote signals or barrier semaphores. Data moves between devices by JAX's collectives and lax.ppermute only.
A program may use at most 192 MiB of HBM per device.

v0:
```python
import jax
import jax.numpy as jnp
from jax import lax
from jax.sharding import PartitionSpec as P

D = 128
TILE = 128


def user_terms(values, tile_row, tile_col, live_mask, items_here, user_blocks):
    slot_total = values.shape[0]
    forward_prod = jnp.einsum(
        "tab,tbd->tad", values, items_here[tile_col], preferred_element_type=jnp.float32
    )
    masked = forward_prod.reshape(slot_total, -1) * live_mask[:, None]
    return jnp.zeros((user_blocks, masked.shape[1]), jnp.float32).at[tile_row].add(masked)


def item_terms(values, tile_row, tile_col, live_mask, users_here, item_blocks):
    slot_total = values.shape[0]
    backward_prod = jnp.einsum(
        "tab,tad->tbd", values, users_here[tile_row], preferred_element_type=jnp.float32
    )
    masked = backward_prod.reshape(slot_total, -1) * live_mask[:, None]
    return jnp.zeros((item_blocks, masked.shape[1]), jnp.float32).at[tile_col].add(masked)


def local(item_embed, item_degree, cotangent, user_degree, tile_values, tile_slots, tile_count):
    n_row = lax.axis_size("row")
    n_col = lax.axis_size("col")
    rows_dev = item_embed.shape[0]
    panel_items = rows_dev * n_row
    panel_users = rows_dev * n_col
    item_blocks = panel_items // TILE
    user_blocks = panel_users // TILE
    values = tile_values[0]
    slot_ids = tile_slots[0]
    live_count = tile_count[0]
    slot_total = values.shape[0]
    inv_item = lax.rsqrt(item_degree.astype(jnp.float32))
    inv_user = lax.rsqrt(user_degree.astype(jnp.float32))
    item_panel = (item_embed * inv_item[:, None]).astype(jnp.bfloat16)
    user_panel = (cotangent * inv_user[:, None]).astype(jnp.bfloat16)
    items_here = lax.all_gather(item_panel, "row", axis=0, tiled=True).reshape(item_blocks, TILE, D)
    users_here = lax.all_gather(user_panel, "col", axis=0, tiled=True).reshape(user_blocks, TILE, D)
    tile_row = slot_ids // item_blocks
    tile_col = slot_ids % item_blocks
    live_mask = (jnp.arange(slot_total, dtype=jnp.int32) < live_count).astype(jnp.float32)
    user_sum = lax.psum_scatter(
        user_terms(values, tile_row, tile_col, live_mask, items_here, user_blocks).reshape(
            panel_users, D
        ),
        "col",
        scatter_dimension=0,
        tiled=True,
    )
    item_sum = lax.psum_scatter(
        item_terms(values, tile_row, tile_col, live_mask, users_here, item_blocks).reshape(
            panel_items, D
        ),
        "row",
        scatter_dimension=0,
        tiled=True,
    )
    return (user_sum * inv_user[:, None], item_sum * inv_item[:, None])


def solution(mesh):
    in_specs = (
        P(("col", "row"), None),
        P(("col", "row")),
        P(("row", "col"), None),
        P(("row", "col")),
        P(("row", "col"), None, None, None),
        P(("row", "col"), None),
        P(("row", "col")),
    )
    out_specs = (P(("row", "col"), None), P(("col", "row"), None))
    return jax.shard_map(local, mesh=mesh, in_specs=in_specs, out_specs=out_specs, check_vma=False)
```

profile of v0, /device:TPU:0, one launch (start us, length us, event | category | flops | bytes accessed | tf_op | source)
XLA Modules:
  0.0 584.2 jit_solution(15623043943250060768)
XLA Ops:
  7.2 0.0 all-gather.5.cloned.1.call-start
  7.2 0.7 convert_rsqrt_fusion
  7.9 2.0 multiply_convert_fusion
  9.9 0.0 all-gather.5.cloned.1.call-update
  9.9 0.0 reduce-scatter.5.cloned.1.call-start
  10.6 0.7 fusion.16
  11.3 56.3 %all-gather.5.cloned.1.call-done = bf16[8192,128]{1,0:T(8,128)(2,1)} async-done(((bf16[1024,128]{1,0:T(8,128)(2,1)}), bf16[8192,128]{1,0:T(8,128)(2,1)}) %all-gather.5.cloned.1.call-update) | async-done | bytes 2097168 | tf_op jit(solution)/shard_map/all_gather | solution.py:45
  67.6 13.0 %gather_fusion.1 = bf16[384,128,128]{2,1,0:T(8,128)(2,1)} fusion(bf16[64,128,128]{2,1,0:T(8,128)(2,1)} %bitcast.40, s32[1024]{0:T(1024)S(1)} %pad_clamp_fusion), kind=kCustom, calls=%fused_computation.1 | custom fusion | bytes 25167360 | tf_op jit(solution)/shard_map/gather | solution.py:22
  80.5 19.1 %fusion.7 = f32[384,128,128]{1,2,0:T(8,128)} fusion(bf16[384,128,128]{2,1,0:T(8,128)(2,1)} %gather_fusion.1, bf16[1,384,128,128]{3,2,1,0:T(8,128)(2,1)} %param.11), kind=kOutput, calls=%fused_computation.11 | convolution fusion | flops 1610612736 | bytes 50331648 | tf_op jit(solution)/shard_map/tab,tad->tbd/dot_general | solution.py:21
  99.6 24.9 %copy.17 = f32[384,128,128]{0,2,1:T(8,128)} copy(f32[384,128,128]{1,2,0:T(8,128)} %fusion.7) | data formatting | bytes 50331648 | tf_op jit(solution)/shard_map/tab,tad->tbd/dot_general | solution.py:21
  124.6 17.1 %bitcast_multiply_fusion = f32[384,16384]{0,1:T(8,128)} fusion(f32[384,128,128]{0,2,1:T(8,128)} %copy.17, f32[384]{0:T(512)S(1)} %fusion.14), kind=kLoop, calls=%fused_computation.4 | loop fusion | flops 6291456 | bytes 50333184 | tf_op jit(solution)/shard_map/mul | solution.py:24
  141.7 24.6 %copy.18 = f32[384,16384]{1,0:T(8,128)} copy(f32[384,16384]{0,1:T(8,128)} %bitcast_multiply_fusion) | data formatting | bytes 50331648 | tf_op jit(solution)/shard_map/mul | solution.py:24
  166.3 39.7 %scatter_custom_fusion.1 = f32[128,16384]{1,0:T(8,128)} fusion(s32[384]{0:T(512)S(1)} %get-tuple-element.2, f32[384,16384]{1,0:T(8,128)} %copy.18, f32[]{:T(128)} %constant.27.clone.1), kind=kCustom, calls=%fused_computation.12 | custom fusion | flops 6291456 | bytes 8389120 | tf_op jit(solution)/shard_map/scatter-add | solution.py:25
  206.0 9.3 %reshape.154 = f32[16384,128]{1,0:T(8,128)} reshape(f32[128,16384]{1,0:T(8,128)} %scatter_custom_fusion.1) | data formatting | bytes 16777216 | tf_op jit(solution)/shard_map/reshape | solution.py:58
  215.3 0.0 reduce-scatter.5.cloned.1.call-update
  215.3 0.0 all-gather.3.cloned.1.call-start
  215.4 0.0 copy-done.1
  215.4 72.5 %reduce-scatter.5.cloned.1.call-done = f32[1024,128]{1,0:T(8,128)} async-done(((f32[16384,128]{1,0:T(8,128)}), f32[1024,128]{1,0:T(8,128)}) %reduce-scatter.5.cloned.1.call-update) | async-done | bytes 524304 | tf_op jit(solution)/shard_map/reduce_scatter | solution.py:57
  287.9 2.1 broadcast_multiply_fusion.1
  290.0 0.0 all-gather.3.cloned.1.call-update
  290.0 0.0 reduce-scatter.3.cloned.1.call-start
  290.1 36.0 %all-gather.3.cloned.1.call-done = bf16[16384,128]{1,0:T(8,128)(2,1)} async-done(((bf16[1024,128]{1,0:T(8,128)(2,1)}), bf16[16384,128]{1,0:T(8,128)(2,1)}) %all-gather.3.cloned.1.call-update) | async-done | bytes 4194320 | tf_op jit(solution)/shard_map/all_gather | solution.py:44
  326.1 13.6 %gather_fusion = bf16[384,128,128]{2,1,0:T(8,128)(2,1)} fusion(bf16[128,128,128]{2,1,0:T(8,128)(2,1)} %bitcast.41, s32[1024]{0:T(1024)S(1)} %pad_clamp_fusion.1), kind=kCustom, calls=%fused_computation | custom fusion | bytes 25167360 | tf_op jit(solution)/shard_map/gather | solution.py:13
  339.6 22.1 %fusion.4 = f32[384,128,128]{1,2,0:T(8,128)} fusion(bf16[384,128,128]{2,1,0:T(8,128)(2,1)} %gather_fusion, bf16[1,384,128,128]{3,2,1,0:T(8,128)(2,1)} %param.11), kind=kOutput, calls=%fused_computation.10 | convolution fusion | flops 1610612736 | bytes 50331648 | tf_op jit(solution)/shard_map/tab,tbd->tad/dot_general | solution.py:12
  361.7 24.9 %copy.14 = f32[384,128,128]{0,2,1:T(8,128)} copy(f32[384,128,128]{1,2,0:T(8,128)} %fusion.4) | data formatting | bytes 50331648 | tf_op jit(solution)/shard_map/tab,tbd->tad/dot_general | solution.py:12
  386.6 17.1 %bitcast_multiply_fusion.1 = f32[384,16384]{0,1:T(8,128)} fusion(f32[384,128,128]{0,2,1:T(8,128)} %copy.14, f32[384]{0:T(512)S(1)} %fusion.14), kind=kLoop, calls=%fused_computation.5 | loop fusion | flops 6291456 | bytes 50333184 | tf_op jit(solution)/shard_map/mul | solution.py:15
  403.7 24.6 %copy.15 = f32[384,16384]{1,0:T(8,128)} copy(f32[384,16384]{0,1:T(8,128)} %bitcast_multiply_fusion.1) | data formatting | bytes 50331648 | tf_op jit(solution)/shard_map/mul | solution.py:15
  428.3 57.3 %scatter_custom_fusion = f32[64,16384]{1,0:T(8,128)} fusion(s32[384]{0:T(512)S(1)} %get-tuple-element.3, f32[384,16384]{1,0:T(8,128)} %copy.15, f32[]{:T(128)} %constant.27.clone.1), kind=kCustom, calls=%fused_computation.14 | custom fusion | flops 6291456 | bytes 4194816 | tf_op jit(solution)/shard_map/scatter-add | solution.py:16
  485.7 4.9 reshape.151
  490.6 0.0 reduce-scatter.3.cloned.1.call-update
  490.6 84.8 %reduce-scatter.3.cloned.1.call-done = f32[1024,128]{1,0:T(8,128)} async-done(((f32[8192,128]{1,0:T(8,128)}), f32[1024,128]{1,0:T(8,128)}) %reduce-scatter.3.cloned.1.call-update) | async-done | bytes 524304 | tf_op jit(solution)/shard_map/reduce_scatter | solution.py:49
  575.4 2.0 broadcast_multiply_fusion
  (7 shorter events, 0.0 us)
Async XLA Ops:
  7.2 60.4 %all-gather.5.cloned.1.call-start = ((), (), s32[]{:S(2)}) async-start(), calls=%async_computation.4 | async-start | bytes 2359296 | tf_op jit(solution)/shard_map/all_gather | solution.py:45
  9.9 278.0 %reduce-scatter.5.cloned.1.call-start = ((), (), s32[]{:S(2)}) async-start(), calls=%async_computation.5 | async-start | bytes 8912896 | tf_op jit(solution)/shard_map/reduce_scatter | solution.py:57
  206.0 9.4 %copy-start.1 = (s32[1024]{0:T(1024)S(1)}, s32[1024]{0:T(1024)}, u32[]{:S(2)}) copy-start(s32[1024]{0:T(1024)} %param.8) | copy-start | bytes 12292
  206.0 81.9 %copy-start = (f32[1024,128]{1,0:T(8,128)S(1)}, f32[1024,128]{1,0:T(8,128)}, u32[]{:S(2)}) copy-start(f32[1024,128]{1,0:T(8,128)} %param.7) | copy-start | bytes 1572868
  215.3 110.7 %all-gather.3.cloned.1.call-start = ((), (), s32[]{:S(2)}) async-start(), calls=%async_computation.2 | async-start | bytes 4456448 | tf_op jit(solution)/shard_map/all_gather | solution.py:44
  290.0 285.4 %reduce-scatter.3.cloned.1.call-start = ((), (), s32[]{:S(2)}) async-start(), calls=%async_computation.3 | async-start | bytes 4718592 | tf_op jit(solution)/shard_map/reduce_scatter | solution.py:49
Sparse Core Ops, SparseCore 0:
  10.9 56.5 all-gather.4
  215.5 72.3 reduce-scatter.4
  290.2 35.8 all-gather.2
  490.7 84.6 reduce-scatter.2
where the time goes:
time: 591 us; the launch traced here: 584 us
  waiting for transfers between devices  250 us (42%)
  local copies, waits for them, and re-layouts  140 us (24%)
  other arithmetic  139 us (24%)
  matrix products  41.2 us (7%)
  between operations  14.6 us (2%)
    reduce_scatter x1, waiting for transfers between devices, local(): lax.psum_scatter(user_terms(values, tile_row, tile_col, live_mask, items_...  84.8 us
    reduce_scatter x1, waiting for transfers between devices, local(): lax.psum_scatter(item_terms(values, tile_row, tile_col, live_mask, users_...  72.5 us
    scatter-add x1, other arithmetic, user_terms(): jnp.zeros((user_blocks, masked.shape[1]), jnp.float32).at[tile_row]  57.3 us
    all_gather x1, waiting for transfers between devices, local(): lax.all_gather(user_panel, 'col', axis=0, tiled=True)  56.3 us
    scatter-add x1, other arithmetic, item_terms(): jnp.zeros((item_blocks, masked.shape[1]), jnp.float32).at[tile_col]  39.7 us
    all_gather x1, waiting for transfers between devices, local(): lax.all_gather(item_panel, 'row', axis=0, tiled=True)  36 us
    dot_general x1, local copies, waits for them, and re-layouts, user_terms(): jnp.einsum('tab,tbd->tad', values, items_here[tile_col], preferred_elemen...  24.9 us
    dot_general x1, local copies, waits for them, and re-layouts, item_terms(): jnp.einsum('tab,tad->tbd', values, users_here[tile_row], preferred_elemen...  24.9 us
  transfers between devices with their start and end apart: 4, of which 4 were waited for; matrix products, arithmetic and copies ran while one was open for 0% of the time, Pallas kernels for 0%

commit v1 on v0

v1 whole, which is shorter than its diff:
```python
import functools

import jax
import jax.numpy as jnp
from jax import lax
from jax.experimental import pallas as pl
from jax.experimental.pallas import tpu as pltpu
from jax.sharding import PartitionSpec as P

D = 128
TILE = 128
CHUNK = 16
UNROLL = 4


def sparse_kernel(transposed, in_blocks, out_blocks, item_blocks, slots_ref, count_ref, values_ref, panel_ref, out_ref, held, acc, sems):
    slot_total = values_ref.shape[0]
    chunks = slot_total // CHUNK
    live = jnp.minimum(count_ref[0], slot_total)
    used = (live + CHUNK - 1) // CHUNK

    def fetch(j):
        start = pl.multiple_of(j * CHUNK, CHUNK)
        return pltpu.make_async_copy(
            values_ref.at[pl.ds(start, CHUNK)], held.at[pl.ds(start, CHUNK)], sems.at[j]
        )

    def start_chunk(j, carry):
        fetch(j).start()
        return carry

    lax.fori_loop(0, used, start_chunk, 0)
    acc[...] = jnp.zeros_like(acc)

    def visit_chunk(j, carry):
        fetch(j).wait()

        def visit(g, inner):
            base = j * CHUNK + g * UNROLL
            prods, places = [], []
            for u in range(UNROLL):
                k = base + u
                slot = slots_ref[0, k]
                row, col = slot // item_blocks, slot % item_blocks
                source, target = (row, col) if transposed else (col, row)
                tile = held[k]
                block = panel_ref[source]
                left, right = (block, tile) if transposed else (tile, block)
                prods.append(jnp.dot(left, right, preferred_element_type=jnp.float32))
                places.append(jnp.where(k < live, target, out_blocks))
            for prod, place in zip(prods, places):
                acc[place] += prod
            return inner

        return lax.fori_loop(0, CHUNK // UNROLL, visit, carry)

    lax.fori_loop(0, used, visit_chunk, 0)

    def finish(i, carry):
        out_ref[i] = acc[i].astype(out_ref.dtype)
        return carry

    lax.fori_loop(0, out_blocks, finish, 0, unroll=4)


def block_sums(transposed, values, slots, count, panel, out_blocks, item_blocks):
    in_blocks = panel.shape[0]
    slot_total = values.shape[0]
    return pl.pallas_call(
        functools.partial(sparse_kernel, transposed, in_blocks, out_blocks, item_blocks),
        out_shape=jax.ShapeDtypeStruct((out_blocks, TILE, D), jnp.bfloat16),
        in_specs=[
            pl.BlockSpec(memory_space=pltpu.SMEM),
            pl.BlockSpec(memory_space=pltpu.SMEM),
            pl.BlockSpec(memory_space=pl.ANY),
            pl.BlockSpec(memory_space=pltpu.VMEM),
        ],
        out_specs=pl.BlockSpec(memory_space=pltpu.VMEM),
        scratch_shapes=[
            pltpu.VMEM((slot_total, TILE, TILE), jnp.bfloat16),
            pltpu.VMEM((out_blocks + 1, TILE, D), jnp.float32),
            pltpu.SemaphoreType.DMA((slot_total // CHUNK,)),
        ],
        compiler_params=pltpu.CompilerParams(vmem_limit_bytes=50 << 20),
        cost_estimate=pl.CostEstimate(
            flops=8 * slot_total * TILE * TILE * D,
            bytes_accessed=slot_total * TILE * TILE * 2 + (in_blocks + out_blocks) * TILE * D * 2,
            transcendentals=0,
        ),
        name="item_sums" if transposed else "user_sums",
    )(slots, count, values, panel)


def local(item_embed, item_degree, cotangent, user_degree, tile_values, tile_slots, tile_count):
    n_row = lax.axis_size("row")
    n_col = lax.axis_size("col")
    own = item_embed.shape[0] // TILE
    item_blocks = own * n_row
    user_blocks = own * n_col
    values = tile_values[0]
    inv_item = lax.rsqrt(item_degree.astype(jnp.float32))
    inv_user = lax.rsqrt(user_degree.astype(jnp.float32))
    item_panel = (item_embed * inv_item[:, None]).astype(jnp.bfloat16).reshape(own, TILE, D)
    user_panel = (cotangent * inv_user[:, None]).reshape(own, TILE, D)
    user_panel = jnp.swapaxes(user_panel, 1, 2).astype(jnp.bfloat16)
    users_here = lax.all_gather(user_panel, "col", axis=0, tiled=True)
    items_here = lax.all_gather(item_panel, "row", axis=0, tiled=True)
    item_part = block_sums(True, values, tile_slots, tile_count, users_here, item_blocks, item_blocks)
    item_part = lax.all_to_all(item_part, "row", 0, 0, tiled=True)
    user_part = block_sums(False, values, tile_slots, tile_count, items_here, user_blocks, item_blocks)
    user_part = lax.all_to_all(user_part, "col", 0, 0, tiled=True)
    item_sum = jnp.sum(item_part.astype(jnp.float32).reshape(n_row, own, D, TILE), axis=0)
    item_sum = jnp.swapaxes(item_sum, 1, 2).reshape(own * TILE, D)
    user_sum = jnp.sum(user_part.astype(jnp.float32).reshape(n_col, own * TILE, D), axis=0)
    return (user_sum * inv_user[:, None], item_sum * inv_item[:, None])


def solution(mesh):
    in_specs = (
        P(("col", "row"), None),
        P(("col", "row")),
        P(("row", "col"), None),
        P(("row", "col")),
        P(("row", "col"), None, None, None),
        P(("row", "col"), None),
        P(("row", "col")),
    )
    out_specs = (P(("row", "col"), None), P(("col", "row"), None))
    return jax.shard_map(local, mesh=mesh, in_specs=in_specs, out_specs=out_specs, check_vma=False)
```

time: 591 us -> 251 us (0.42)
  local copies, waits for them, and re-layouts: 140 us -> 3.34 us
  other arithmetic: 139 us -> 7.34 us
  waiting for transfers between devices: 250 us -> 159 us
  matrix products: 41.2 us -> 0 us
  blocking collectives: 0 us -> 34.6 us
  Pallas kernels: 0 us -> 23.1 us
    reduce_scatter x2 -> x0, waiting for transfers between devices: 157 us -> none  [the longest x1 84.8 us: local(): lax.psum_scatter(user_terms(values, tile_row, tile_col, live_mask, items_...]
    scatter-add x2 -> x0, other arithmetic: 97 us -> none  [the longest x1 57.3 us: user_terms(): jnp.zeros((user_blocks, masked.shape[1]), jnp.float32).at[tile_row]]
    all_to_all x0 -> x1, waiting for transfers between devices: none -> 56.1 us  [local(): item_part = lax.all_to_all(item_part, 'row', 0, 0, tiled=True)]
    dot_general x2 -> x0, local copies, waits for them, and re-layouts: 49.8 us -> none  [the longest x1 24.9 us: user_terms(): jnp.einsum('tab,tbd->tad', values, items_here[tile_col], preferred_elemen...]
    mul x2 -> x0, local copies, waits for them, and re-layouts: 49.2 us -> none  [the longest x1 24.6 us: item_terms(): masked = backward_prod.reshape(slot_total, -1) * live_mask[:, None]]
    dot_general x2 -> x0, matrix products: 41.2 us -> none  [the longest x1 22.1 us: user_terms(): jnp.einsum('tab,tbd->tad', values, items_here[tile_col], preferred_elemen...]
    all_to_all x0 -> x1, blocking collectives: none -> 34.6 us  [local(): user_part = lax.all_to_all(user_part, 'col', 0, 0, tiled=True)]
    mul x2 -> x0, other arithmetic: 34.2 us -> none  [the longest x1 17.1 us: item_terms(): masked = backward_prod.reshape(slot_total, -1) * live_mask[:, None]]
  transfers between devices with their start and end apart: 4 -> 3, of which waited for: 4 -> 3; matrix products, arithmetic and copies ran while one was open for 0% -> 0% of each run, Pallas kernels for 0% -> 0%
where the time goes in v1:
time: 251 us; the launch traced here: 248 us
  waiting for transfers between devices  159 us (63%)
  blocking collectives  34.6 us (14%)
  Pallas kernels  23.1 us (9%)
  between operations  14.8 us (6%)
  other arithmetic  7.34 us (3%)
  starting transfers between devices  5.73 us (2%)
  local copies, waits for them, and re-layouts  3.34 us (1%)
    all_gather x1, waiting for transfers between devices, local(): users_here = lax.all_gather(user_panel, 'col', axis=0, tiled=True)  56.9 us
    all_to_all x1, waiting for transfers between devices, local(): item_part = lax.all_to_all(item_part, 'row', 0, 0, tiled=True)  56.1 us
    all_gather x1, waiting for transfers between devices, local(): items_here = lax.all_gather(item_panel, 'row', axis=0, tiled=True)  45.6 us
    all_to_all x1, blocking collectives, local(): user_part = lax.all_to_all(user_part, 'col', 0, 0, tiled=True)  34.6 us
    pallas_call x2, Pallas kernels, block_sums(): pl.pallas_call(functools.partial(sparse_kernel, transposed, in_blocks, ou...  23.1 us
    all_to_all x1, starting transfers between devices, local(): item_part = lax.all_to_all(item_part, 'row', 0, 0, tiled=True)  5.65 us
  transfers between devices with their start and end apart: 3, of which 3 were waited for; matrix products, arithmetic and copies ran while one was open for 0% of the time, Pallas kernels for 0%

profile of v1, /device:TPU:0, one launch (start us, length us, event | category | flops | bytes accessed | tf_op | source)
XLA Modules:
  0.0 247.6 jit_solution(757461061420871790)
XLA Ops:
  7.2 0.0 all-gather.5.cloned.1.call-start
  7.2 0.7 convert_rsqrt_fusion
  7.9 1.2 multiply_convert_fusion
  9.2 0.9 copy.11
  10.0 0.0 all-gather.5.cloned.1.call-update
  10.7 56.9 %all-gather.5.cloned.1.call-done.panel_ref = bf16[64,128,128]{2,1,0:T(8,128)(2,1)} async-done(((bf16[8,128,128]{2,1,0:T(8,128)(2,1)}), bf16[64,128,128]{2,1,0:T(8,128)(2,1)}) %all-gather.5.cloned.1.call-update) | async-done | bytes 2097168 | tf_op jit(solution)/shard_map/all_gather | solution.py:106
  67.6 0.0 copy-start
  67.6 1.6 copy-done
  69.2 0.0 copy-start.1
  69.2 0.7 copy-done.1
  69.8 11.7 %item_sums.1 = bf16[128,128,128]{2,1,0:T(8,128)(2,1)} custom-call(s32[1,384]{1,0:T(1,128)S(1)} %copy-done.1, s32[1]{0:T(128)S(6)} %copy.13.count_ref, bf16[384,128,128]{2,1,0:T(8,128)(2,1)} %bitcast.18, bf16[64,128,128]{2,1,0:T(8,128)(2,1)S(1)} %copy-done), custom_call_target="tpu_custom_call" | custom-call | flops 6442450944 | bytes 18874368 | tf_op jit(solution)/shard_map/item_sums/pallas_call | solution.py:69
  81.5 0.0 copy-start.4
  81.5 5.7 %all-to-all-start.1 = ((bf16[128,128,128]{2,1,0:T(8,128)(2,1)}), bf16[128,128,128]{2,1,0:T(8,128)(2,1)}, u32[]{:S(2)}, u32[]{:S(2)}) async-start(bf16[128,128,128]{2,1,0:T(8,128)(2,1)} %item_sums.1), calls=%async_computation.1 | async-start | bytes 8388608 | tf_op jit(solution)/shard_map/all_to_all | solution.py:109
  87.2 0.0 copy-start.3
  87.2 0.0 copy-start.2
  87.2 0.0 all-gather.3.cloned.1.call-start
  87.3 0.0 copy-done.4
  87.3 56.1 %all-to-all-done.1 = bf16[128,128,128]{2,1,0:T(8,128)(2,1)} async-done(((bf16[128,128,128]{2,1,0:T(8,128)(2,1)}), bf16[128,128,128]{2,1,0:T(8,128)(2,1)}, u32[]{:S(2)}, u32[]{:S(2)}) %all-to-all-start.1) | async-done | bytes 4194336 | tf_op jit(solution)/shard_map/all_to_all | solution.py:109
  143.4 3.0 %convert_reduce_fusion = f32[8,128,128]{2,1,0:T(8,128)S(1)} fusion(bf16[16,8,128,128]{3,2,1,0:T(8,128)(2,1)} %bitcast.10), kind=kLoop, calls=%fused_computation | loop fusion | flops 4063232 | bytes 4718592 | tf_op jit(solution)/shard_map/reduce_sum | solution.py:112
  146.4 0.2 copy.12
  146.6 0.0 copy-done.3
  146.6 1.1 bitcast_multiply_fusion
  147.7 0.0 all-gather.3.cloned.1.call-update
  147.7 45.6 %all-gather.3.cloned.1.call-done.panel_ref = bf16[128,128,128]{2,1,0:T(8,128)(2,1)} async-done(((bf16[8,128,128]{2,1,0:T(8,128)(2,1)}), bf16[128,128,128]{2,1,0:T(8,128)(2,1)}) %all-gather.3.cloned.1.call-update) | async-done | bytes 4194320 | tf_op jit(solution)/shard_map/all_gather | solution.py:107
  193.4 0.0 copy-done.2
  193.4 11.5 %user_sums.1 = bf16[64,128,128]{2,1,0:T(8,128)(2,1)S(1)} custom-call(s32[1,384]{1,0:T(1,128)S(1)} %copy-done.2, s32[1]{0:T(128)S(6)} %copy.13.count_ref, bf16[384,128,128]{2,1,0:T(8,128)(2,1)} %bitcast.19, bf16[128,128,128]{2,1,0:T(8,128)(2,1)} %all-gather.3.cloned.1.call-done.panel_ref), custom_call_target="tpu_custom_call" | custom-call | flops 6442450944 | bytes 18874368 | tf_op jit(solution)/shard_map/user_sums/pallas_call | solution.py:69
  204.9 34.6 %all_to_all.10 = bf16[64,128,128]{2,1,0:T(8,128)(2,1)S(1)} all-to-all(bf16[64,128,128]{2,1,0:T(8,128)(2,1)S(1)} %user_sums.1), channel_id=1, replica_groups=mesh['row'=16,'col'=8] {'col'}, dimensions={0} | all-to-all | bytes 4194304 | tf_op jit(solution)/shard_map/all_to_all | solution.py:111
  239.5 0.3 convert_reduce_fusion.1
  239.8 1.0 broadcast_multiply_fusion
  (1 shorter events, 0.0 us)
Async XLA Ops:
  7.2 60.4 %all-gather.5.cloned.1.call-start = ((), (), s32[]{:S(2)}) async-start(), calls=%async_computation.3 | async-start | bytes 2359296 | tf_op jit(solution)/shard_map/all_gather | solution.py:106
  67.6 1.6 copy-start
  69.2 0.7 copy-start.1
  81.5 5.7 %copy-start.4 = (s32[1024]{0:T(1024)S(1)}, s32[1024]{0:T(1024)}, u32[]{:S(2)}) copy-start(s32[1024]{0:T(1024)} %param.8) | copy-start | bytes 12292
  81.5 61.9 %all-to-all-start.1 = ((bf16[128,128,128]{2,1,0:T(8,128)(2,1)}), bf16[128,128,128]{2,1,0:T(8,128)(2,1)}, u32[]{:S(2)}, u32[]{:S(2)}) async-start(bf16[128,128,128]{2,1,0:T(8,128)(2,1)} %item_sums.1), calls=%async_computation.1 | async-start | bytes 8388608 | tf_op jit(solution)/shard_map/all_to_all | solution.py:109
  87.2 59.5 %copy-start.3 = (f32[1024,128]{1,0:T(8,128)S(1)}, f32[1024,128]{1,0:T(8,128)}, u32[]{:S(2)}) copy-start(f32[1024,128]{1,0:T(8,128)} %param.7) | copy-start | bytes 1572868
  87.2 106.2 %copy-start.2 = (s32[1,384]{1,0:T(1,128)S(1)}, s32[1,384]{1,0:T(1,128)}, u32[]{:S(2)}) copy-start(s32[1,384]{1,0:T(1,128)} %slots_ref.3) | copy-start | bytes 4612
  87.2 106.2 %all-gather.3.cloned.1.call-start = ((), (), s32[]{:S(2)}) async-start(), calls=%async_computation.2 | async-start | bytes 4456448 | tf_op jit(solution)/shard_map/all_gather | solution.py:107
Sparse Core Ops, SparseCore 0:
  10.9 56.5 all-gather.4
  147.9 45.4 all-gather.2
